TPU v7x, 32 devices: a whole 2x2x4 slice. The times are simulated.
32 devices in a mesh: gx: 4 (over x, core), gy: 8 (over z, y).
Axes of the slice: x: 2, y: 2, z: 4, core: 2. Of those that a mesh axis runs over, the one named last changes fastest.
Arguments:
- populations: float32 [19, 64, 128, 128], P(None, 'gx', 'gy'), may hold values from 0.02 to 0.1
- porosity: float32 [64, 128, 128], P('gx', 'gy'), may hold values from 0.05 to 0.95
- adjoint_in: float32 [19, 64, 128, 128], P(None, 'gx', 'gy'), may hold values from -6 to 6
- porous: int32 [64, 128, 128], P('gx', 'gy'), may hold values 0 or 1
- walls: int32 [64, 128, 128], P('gx', 'gy'), may hold values 0 or 1
- owners: int32 [4, 8, 64, 1], P('gx', 'gy'), may hold values from 0 to 31; in each aligned block of 64 rows (0 to 63, 64 to 127, ..., all dimensions but the last counted through in order) at most 4 rows name the same one
- slots: int32 [4, 8, 64], P('gx', 'gy'), may hold values from 0 to 255
Outputs:
- adjoint_out: float32 [19, 64, 128, 128], P(None, 'gx', 'gy')
- patch_sens: float32 [8192], P(('gx', 'gy'))
Inputs may be any that keep to these rules, and one draw needn't show every extreme that they name: `owners`: of the 64 panel blocks of one device, at most 4 name the same owner device, and some device's blocks reach 4 for some owner in every draw.
All inputs are finite; a program needn't handle non-finite values. No bound on the sum of `porous` or of `walls` on one device may be relied on, other than what follows from the above.
Results may differ from a plain program's by a relative error of at most 0.0003.
Values sent between devices are 32-bit elements; how exact they have to be, the bound alone decides.
A program may use at most 128 MiB of HBM per device.

v0:
```python
from functools import partial

import jax
import jax.numpy as jnp
from jax import lax
from jax.experimental import pallas as pl
from jax.experimental.pallas import tpu as pltpu
from jax.sharding import PartitionSpec as P

PATCH_DEV = 256
MESH = pl.DeviceIdType.MESH

VELOCITIES = [
    (0, 0, 0),
    (1, 0, 0), (-1, 0, 0), (0, 1, 0), (0, -1, 0), (0, 0, 1), (0, 0, -1),
    (1, 1, 0), (-1, -1, 0), (1, -1, 0), (-1, 1, 0),
    (1, 0, 1), (-1, 0, -1), (1, 0, -1), (-1, 0, 1),
    (0, 1, 1), (0, -1, -1), (0, 1, -1), (0, -1, 1),
]
ORDER = [0, 3, 4, 5, 6, 15, 16, 17, 18, 1, 7, 9, 11, 13, 2, 8, 10, 12, 14]
POS = [ORDER.index(i) for i in range(19)]
X_START = {1: 9, -1: 14}
Y_GROUP = {1: [3, 7, 10, 15, 17], -1: [4, 8, 9, 16, 18]}
CORNERS = [(1, 1), (-1, -1), (1, -1), (-1, 1)]
CORNER_POP = {(1, 1): 7, (-1, -1): 8, (1, -1): 9, (-1, 1): 10}
PLANES = (7, 11, 15)
RATE2, RATE3, RATE4 = 1.25, 1.5, 1.4


def split_planes(f):
    out = []
    for start in PLANES:
        a, b, c, d = f[start : start + 4]
        s1, s2, t1, t2 = a + b, c + d, a - b, c - d
        out.append((s1 + s2, s1 - s2, t1 + t2, t1 - t2, t1, t2))
    return out


def split_faces(f):
    return [f[1] + f[2], f[3] + f[4], f[5] + f[6]], [f[1] - f[2], f[3] - f[4], f[5] - f[6]]


def nonequilibrium(f):
    (w_xy, w_xz, w_yz) = planes = split_planes(f)
    sums, diffs = split_faces(f)
    second = [sums[0] + w_xy[0] + w_xz[0], sums[1] + w_xy[0] + w_yz[0], sums[2] + w_xz[0] + w_yz[0]]
    jx = diffs[0] + (w_xy[2] + w_xz[2])
    jy = diffs[1] + (w_xy[3] + w_yz[2])
    jz = diffs[2] + (w_xz[3] + w_yz[3])
    rho = (f[0] + sums[0]) + (sums[1] + sums[2]) + ((w_xy[0] + w_xz[0]) + w_yz[0])
    inverse = 1.0 / rho
    ux, uy, uz = jx * inverse, jy * inverse, jz * inverse
    qx, qy, qz = jx * ux, jy * uy, jz * uz
    third_rho = rho * (1.0 / 3.0)
    second = [second[0] - third_rho - qx, second[1] - third_rho - qy, second[2] - third_rho - qz]
    product = [w_xy[1] - jx * uy, w_xz[1] - jx * uz, w_yz[1] - jy * uz]
    kx, ky, kz = jx * (1.0 / 3.0), jy * (1.0 / 3.0), jz * (1.0 / 3.0)
    first = [w_xy[2] - kx, w_xz[2] - kx, w_yz[2] - ky]
    other = [w_xy[3] - ky, w_xz[3] - kz, w_yz[3] - kz]
    base = rho * (1.0 / 9.0) + ((qx + qy) + qz) * (1.0 / 3.0)
    fourth = [w_xy[0] - base + 0.5 * qz, w_xz[0] - base + 0.5 * qy, w_yz[0] - base + 0.5 * qx]
    return planes, diffs, (ux, uy, uz), (second, product, first, other, fourth)


def forward(f, phi):
    _, _, _, (second, product, first, other, fourth) = nonequilibrium(f)
    second = [v * (0.5 * RATE2) for v in second]
    product = [v * (0.25 * RATE2) for v in product]
    first = [v * (0.25 * RATE3) for v in first]
    other = [v * (0.25 * RATE3) for v in other]
    fourth = [v * (0.25 * RATE4) for v in fourth]
    change = [None] * 19
    change[0] = 4.0 * (fourth[0] + fourth[1] + fourth[2]) - 2.0 * (second[0] + second[1] + second[2])
    evens = [
        second[0] - 2.0 * (fourth[0] + fourth[1]),
        second[1] - 2.0 * (fourth[0] + fourth[2]),
        second[2] - 2.0 * (fourth[1] + fourth[2]),
    ]
    odds = [
        2.0 * (first[0] + first[1]),
        2.0 * (other[0] + first[2]),
        2.0 * (other[1] + other[2]),
    ]
    for axis in range(3):
        change[1 + 2 * axis] = evens[axis] - odds[axis]
        change[2 + 2 * axis] = evens[axis] + odds[axis]
    for plane, start in enumerate(PLANES):
        h, k = fourth[plane] + product[plane], fourth[plane] - product[plane]
        p, q = first[plane] + other[plane], first[plane] - other[plane]
        change[start : start + 4] = [h + p, h - p, k + q, k - q]
    relaxed = [f[i] - change[i] for i in range(19)]
    opposite = [0] + [i + 1 if i % 2 else i - 1 for i in range(1, 19)]
    return [relaxed[i] + phi * (f[opposite[i]] - relaxed[i]) for i in range(19)]


def backward(f, a, phi):
    f_planes, f_diffs, (ux, uy, uz), moments = nonequilibrium(f)
    a_planes = split_planes(a)
    a_sums, a_diffs = split_faces(a)
    half = [0.5 * v for v in a_sums]
    n_xy, n_xz, n_yz = a_planes
    b2 = [RATE2 * (v - a[0]) for v in half]
    b11 = [(0.25 * RATE2) * n[1] for n in a_planes]
    hx, hy, hz = [(0.5 * RATE3) * v for v in a_diffs]
    b_first = [
        (0.25 * RATE3) * n_xy[2] - hx, (0.25 * RATE3) * n_xz[2] - hx, (0.25 * RATE3) * n_yz[2] - hy
    ]
    b_other = [
        (0.25 * RATE3) * n_xy[3] - hy, (0.25 * RATE3) * n_xz[3] - hz, (0.25 * RATE3) * n_yz[3] - hz
    ]
    b4 = [
        RATE4 * (0.25 * n_xy[0] - (half[0] + half[1]) + a[0]),
        RATE4 * (0.25 * n_xz[0] - (half[0] + half[2]) + a[0]),
        RATE4 * (0.25 * n_yz[0] - (half[1] + half[2]) + a[0]),
    ]
    sens = None
    for mine, theirs in zip((b2, b11, b_first, b_other, b4), moments):
        for v, m in zip(mine, theirs):
            sens = v * m if sens is None else sens + v * m
    for axis in range(3):
        sens = sens - f_diffs[axis] * a_diffs[axis]
    for p, n in zip(f_planes, a_planes):
        sens = sens - p[4] * n[4] - p[5] * n[5]

    keep = 1.0 - phi
    b2, b11, b_first, b_other, b4 = [
        [keep * v for v in part] for part in (b2, b11, b_first, b_other, b4)
    ]
    total4 = b4[0] + b4[1] + b4[2]
    twice = total4 * (2.0 / 3.0)
    cx, cy, cz = 2.0 * b2[0] + twice - b4[2], 2.0 * b2[1] + twice - b4[1], 2.0 * b2[2] + twice - b4[0]
    wx = cx * ux + b11[0] * uy + b11[1] * uz
    wy = cy * uy + b11[0] * ux + b11[2] * uz
    wz = cz * uz + b11[1] * ux + b11[2] * uy
    r0 = (
        0.5 * (ux * wx + uy * wy + uz * wz)
        - (b2[0] + b2[1] + b2[2]) * (1.0 / 3.0)
        - total4 * (1.0 / 9.0)
    )
    rx = -(b_first[0] + b_first[1]) * (1.0 / 3.0) - wx
    ry = -(b_other[0] + b_first[2]) * (1.0 / 3.0) - wy
    rz = -(b_other[1] + b_other[2]) * (1.0 / 3.0) - wz
    result = [None] * 19
    result[0] = a[0] - r0
    evens = [r0 + b2[0], r0 + b2[1], r0 + b2[2]]
    for axis, odd in enumerate((rx, ry, rz)):
        back = phi * a_diffs[axis] + odd
        result[1 + 2 * axis] = (a[1 + 2 * axis] - evens[axis]) - back
        result[2 + 2 * axis] = (a[2 + 2 * axis] - evens[axis]) + back
    for plane, (start, one, two) in enumerate(((7, 0, 1), (11, 0, 2), (15, 1, 2))):
        even = evens[one] + b2[two] + b4[plane]
        p = (rx, ry, rz)[one] + b_first[plane]
        q = (rx, ry, rz)[two] + b_other[plane]
        h, k = even + b11[plane], even - b11[plane]
        s = (p + q) + phi * a_planes[plane][4]
        t = (p - q) + phi * a_planes[plane][5]
        result[start] = (a[start] - h) - s
        result[start + 1] = (a[start + 1] - h) + s
        result[start + 2] = (a[start + 2] - k) - t
        result[start + 3] = (a[start + 3] - k) + t
    return result, sens


def kernel(
    sizes, pops_hbm, porosity_hbm, adj_hbm, porous_hbm, walls_hbm, ids_ref, out_hbm, patch_ref,
    pops, porosity, adj, porous, walls, out, ahead, behind, late_sens, early_sens,
    y_send, y_recv, c_send, c_recv, message, gathered,
    load_sem, store_sem, halo_send, halo_recv, patch_send, patch_recv,
):
    n_gx, n_gy, cx, cy, nz = sizes
    n = n_gx * n_gy
    stride = cy + 16
    gx, gy = lax.axis_index("gx"), lax.axis_index("gy")
    me = gx * n_gy + gy

    loads = [
        pltpu.make_async_copy(src, dst, load_sem.at[k])
        for k, (src, dst) in enumerate((
            (porosity_hbm, porosity), (porous_hbm, porous), (walls_hbm, walls),
            (pops_hbm, pops), (adj_hbm, adj),
        ))
    ]
    for load in loads:
        load.start()

    def place(k):
        index = lax.rem(me + k, n)
        return (index // n_gy, lax.rem(index, n_gy))

    barrier = pltpu.get_barrier_semaphore()

    @pl.loop(1, n)
    def _(k):
        pl.semaphore_signal(barrier, inc=1, device_id=place(k), device_id_type=MESH)

    def near(dx, dy):
        return (lax.rem(gx + (dx + n_gx), n_gx), lax.rem(gy + (dy + n_gy), n_gy))

    def spin(value, shift):
        return value if shift == 0 else pltpu.roll(value, shift % nz, 1)

    def window(x, y, along_x):
        return pl.ds(x * cy + y, 8, stride=cy) if along_x else pl.ds(x * cy + y, 8)

    def shifted(x, y, i, sign, along_x):
        ex, ey, _ = VELOCITIES[i]
        row = (x + 1 - sign * ex) * stride + 8 + y - sign * ey
        return pl.ds(row, 8, stride=stride) if along_x else pl.ds(row, 8)

    def padded(x, y, along_x):
        row = (x + 1) * stride + 8 + y
        return pl.ds(row, 8, stride=stride) if along_x else pl.ds(row, 8)

    def fractions(rows):
        porous_here = porous[rows, :].astype(jnp.float32)
        wall = walls[rows, :] == 1
        phi = jnp.where(wall, 1.0, porous_here * porosity[rows, :])
        return phi, jnp.where(wall, 0.0, porous_here)

    def pack(stage, values, x, y, sign):
        side = 1 if y else -1
        which = 0 if side > 0 else 1
        for k, i in enumerate(Y_GROUP[side * sign]):
            y_send[stage, which, k, pl.ds(x, 8), :] = values[i]
        for number, (sx, sy) in enumerate(CORNERS):
            if sy == side and x == (cx - 8 if sx > 0 else 0):
                value = values[CORNER_POP[(sx * sign, sy * sign)]]
                row = 7 if sx > 0 else 0
                c_send[stage, number, :, :] = value[row : row + 1, :]

    def step_one(x, y, along_x):
        rows = window(x, y, along_x)
        f = [pops[i, rows, :] for i in range(19)]
        phi, _ = fractions(rows)
        values = [spin(v, VELOCITIES[i][2]) for i, v in enumerate(forward(f, phi))]
        if along_x:
            pack(0, values, x, y, 1)
        else:
            for i in range(19):
                ahead[POS[i], padded(x, y, False), :] = values[i]

    def step_two(x, y, along_x):
        rows = window(x, y, along_x)
        f = [ahead[POS[i], shifted(x, y, i, 1, along_x), :] for i in range(19)]
        a = [adj[i, rows, :] for i in range(19)]
        phi, weight = fractions(rows)
        values, sens = backward(f, a, phi)
        values = [spin(v, -VELOCITIES[i][2]) for i, v in enumerate(values)]
        late_sens[rows, :] = weight * sens
        if along_x:
            pack(1, values, x, y, -1)
        for i in range(19):
            behind[POS[i], padded(x, y, along_x), :] = values[i]

    def step_three(x, y, along_x):
        rows = window(x, y, along_x)
        f = [pops[i, rows, :] for i in range(19)]
        a = [behind[POS[i], shifted(x, y, i, -1, along_x), :] for i in range(19)]
        phi, weight = fractions(rows)
        values, sens = backward(f, a, phi)
        early_sens[rows, :] = weight * sens
        for i in range(19):
            out[i, rows, :] = values[i]

    def y_edges(step):
        for y in (0, cy - 1):
            for x in range(0, cx, 8):
                step(x, y, True)

    def x_faces(step):
        for x in (0, cx - 1):
            for y in range(0, cy, 8):
                step(x, y, False)

    def inner(step):
        @pl.loop(1, cx - 1)
        def _(x):
            for y in range(0, cy, 8):
                step(x, y, False)

    def send(stage, number, src, dst, dx, dy):
        copy = pltpu.make_async_remote_copy(
            src_ref=src, dst_ref=dst,
            send_sem=halo_send.at[stage, number], recv_sem=halo_recv.at[stage, number],
            device_id=near(dx, dy), device_id_type=MESH,
        )
        copy.start()
        return copy

    def send_y(stage):
        copies = [
            send(stage, which, y_send.at[stage, which], y_recv.at[stage, which], 0, side)
            for which, side in enumerate((1, -1))
        ]
        for number, (sx, sy) in enumerate(CORNERS):
            copies.append(
                send(stage, 2 + number, c_send.at[stage, number], c_recv.at[stage, number], sx, sy)
            )
        return copies

    def send_x(stage, buffer, sign):
        copies = []
        for which, side in enumerate((1, -1)):
            group = pl.ds(X_START[side * sign], 5)
            source = (cx if side > 0 else 1) * stride + 8
            target = (0 if side > 0 else cx + 1) * stride + 8
            copies.append(send(
                stage, 6 + which, buffer.at[group, pl.ds(source, cy), :],
                buffer.at[group, pl.ds(target, cy), :], side, 0,
            ))
        return copies

    def receive(stage, copies, buffer, sign):
        for copy in copies:
            copy.wait_recv()
        for which, side in enumerate((1, -1)):
            row = 8 + (-1 if side > 0 else cy)
            for k, i in enumerate(Y_GROUP[side * sign]):
                for x in range(0, cx, 8):
                    buffer[POS[i], pl.ds((x + 1) * stride + row, 8, stride=stride), :] = (
                        y_recv[stage, which, k, pl.ds(x, 8), :]
                    )
        for number, (sx, sy) in enumerate(CORNERS):
            i = CORNER_POP[(sx * sign, sy * sign)]
            row = (0 if sx > 0 else cx + 1) * stride + 8 + (-1 if sy > 0 else cy)
            buffer[POS[i], pl.ds(row, 1), :] = c_recv[stage, number]

    for load in loads[:4]:
        load.wait()
    y_edges(step_one)
    pl.semaphore_wait(barrier, n - 1)
    copies = send_y(0)
    x_faces(step_one)
    copies += send_x(0, ahead, 1)
    inner(step_one)
    loads[4].wait()
    inner(step_two)
    receive(0, copies, ahead, 1)
    y_edges(step_two)
    later = send_y(1)
    x_faces(step_two)
    later += send_x(1, behind, -1)
    inner(step_three)
    receive(1, later, behind, -1)
    y_edges(step_three)
    x_faces(step_three)

    store = pltpu.make_async_copy(out, out_hbm, store_sem)
    store.start()

    rows_of = []
    for x in range(0, cx, 2):
        part = None
        for start in (x * cy, x * cy + 1, (x + 1) * cy, (x + 1) * cy + 1):
            for sens in (late_sens, early_sens):
                piece = sens[pl.ds(start, cy // 2, stride=2), :]
                part = piece if part is None else part + piece
        rows_of.append(part)
    blocks = (cx // 2) * (cy // 2)
    rows_of.append(jnp.zeros((nz - blocks, nz), jnp.float32))
    contract = (((1,), (1,)), ((), ()))
    ones = jnp.ones((8, nz), jnp.float32)
    sums = lax.dot_general(
        ones, jnp.concatenate(rows_of, axis=0), contract,
        precision=lax.Precision.HIGHEST, preferred_element_type=jnp.float32,
    )
    note = sums[0:1, :] + ids_ref[...]
    message[0] = note
    gathered[0] = note

    def patch_copy(k):
        return pltpu.make_async_remote_copy(
            src_ref=message.at[0], dst_ref=gathered.at[k],
            send_sem=patch_send, recv_sem=patch_recv,
            device_id=place(k), device_id_type=MESH,
        )

    @pl.loop(1, n)
    def _(k):
        patch_copy(k).start()

    for copy in copies + later:
        copy.wait_send()
    others = gathered.at[pl.ds(1, n - 1)]
    pltpu.make_async_copy(others, others, patch_recv).wait()

    lane = lax.broadcasted_iota(jnp.int32, (1, nz), 1)
    low = lane < nz // 2
    patch = lax.broadcasted_iota(jnp.int32, (PATCH_DEV, nz), 0).astype(jnp.float32)
    base = (me * PATCH_DEV).astype(jnp.float32)

    def add(k, total):
        one, two = gathered[k], gathered[k + n // 2]
        one_turned, two_turned = pltpu.roll(one, nz // 2, 1), pltpu.roll(two, nz // 2, 1)
        values = jnp.where(low, one, two_turned)
        names = jnp.where(low, one_turned, two) - base
        return total + jnp.where(names == patch, values, 0.0)

    total = lax.fori_loop(0, n // 2, add, jnp.zeros((PATCH_DEV, nz), jnp.float32))
    summed = lax.dot_general(
        ones, total, contract,
        precision=lax.Precision.HIGHEST, preferred_element_type=jnp.float32,
    )
    patch_ref[...] = summed[0:1, :]
    pltpu.make_async_copy(others, others, patch_send).wait()
    store.wait()


def body(sizes, populations, porosity, adjoint_in, porous, walls, owners, slots):
    _, cx, cy, nz = populations.shape
    rows = cx * cy
    n = sizes[0] * sizes[1]
    ids = (owners.reshape(1, -1) * PATCH_DEV + slots.reshape(1, -1)).astype(jnp.float32)
    ids = jnp.concatenate([jnp.zeros((1, nz - ids.shape[1]), jnp.float32), ids], axis=1)
    flat = lambda v: v.reshape(v.shape[:-3] + (rows, nz))
    anywhere = pl.BlockSpec(memory_space=pl.ANY)
    vmem = pl.BlockSpec(memory_space=pltpu.VMEM)
    wide = (19, (cx + 2) * (cy + 16), nz)
    f32 = jnp.float32
    result, patch = pl.pallas_call(
        partial(kernel, (*sizes, cx, cy, nz)),
        out_shape=(
            jax.ShapeDtypeStruct((19, rows, nz), f32), jax.ShapeDtypeStruct((1, PATCH_DEV), f32)
        ),
        in_specs=[anywhere] * 5 + [vmem],
        out_specs=(anywhere, vmem),
        scratch_shapes=[
            pltpu.VMEM((19, rows, nz), f32),
            pltpu.VMEM((rows, nz), f32),
            pltpu.VMEM((19, rows, nz), f32),
            pltpu.VMEM((rows, nz), jnp.int32),
            pltpu.VMEM((rows, nz), jnp.int32),
            pltpu.VMEM((19, rows, nz), f32),
            pltpu.VMEM(wide, f32),
            pltpu.VMEM(wide, f32),
            pltpu.VMEM((rows, nz), f32),
            pltpu.VMEM((rows, nz), f32),
            pltpu.VMEM((2, 2, 5, cx, nz), f32),
            pltpu.VMEM((2, 2, 5, cx, nz), f32),
            pltpu.VMEM((2, 4, 1, nz), f32),
            pltpu.VMEM((2, 4, 1, nz), f32),
            pltpu.VMEM((1, 1, nz), f32),
            pltpu.VMEM((n, 1, nz), f32),
            pltpu.SemaphoreType.DMA((5,)),
            pltpu.SemaphoreType.DMA,
            pltpu.SemaphoreType.DMA((2, 8)),
            pltpu.SemaphoreType.DMA((2, 8)),
            pltpu.SemaphoreType.DMA,
            pltpu.SemaphoreType.DMA,
        ],
        compiler_params=pltpu.CompilerParams(
            collective_id=0, has_side_effects=True, vmem_limit_bytes=40 * 1024 * 1024
        ),
    )(flat(populations), flat(porosity), flat(adjoint_in), flat(porous), flat(walls), ids)
    return result.reshape(populations.shape), patch.reshape(-1)


def solution(mesh):
    sizes = (mesh.shape["gx"], mesh.shape["gy"])
    return jax.shard_map(
        partial(body, sizes),
        mesh=mesh,
        in_specs=(
            P(None, "gx", "gy", None),
            P("gx", "gy", None),
            P(None, "gx", "gy", None),
            P("gx", "gy", None),
            P("gx", "gy", None),
            P("gx", "gy", None, None),
            P("gx", "gy", None),
        ),
        out_specs=(P(None, "gx", "gy", None), P(("gx", "gy"))),
        check_vma=False,
    )
```

profile of v0, /device:TPU:0, one launch (start us, length us, event | category | flops | bytes accessed | tf_op | source)
XLA Modules:
  0.0 35.9 jit_solution(7317736356610106675)
XLA Ops:
  0.6 0.7 %fusion = f32[1,64]{1,0:T(1,128)S(1)} fusion(s32[1,1,64]{2,1,0:T(1,128)} %param.13, s32[1,1,64,1]{2,3,1,0:T(1,128)} %param.12), kind=kLoop, calls=%fused_computation.1 | loop fusion | flops 192 | bytes 768 | tf_op jit(solution)/shard_map/convert_element_type | solution.py:413
  1.3 0.1 concatenate.3.ids_ref
  1.4 0.0 copy-start
  1.4 1.7 %copy-done = f32[19,16,16,128]{3,2,1,0:T(8,128)S(1)} copy-done((f32[19,16,16,128]{3,2,1,0:T(8,128)S(1)}, f32[19,16,16,128]{3,2,1,0:T(8,128)}, u32[]{:S(2)}) %copy-start) | copy-done | bytes 2490392
  3.1 0.0 copy-start.1
  3.1 1.7 %copy-done.1 = f32[19,16,16,128]{3,2,1,0:T(8,128)S(1)} copy-done((f32[19,16,16,128]{3,2,1,0:T(8,128)S(1)}, f32[19,16,16,128]{3,2,1,0:T(8,128)}, u32[]{:S(2)}) %copy-start.1) | copy-done | bytes 2490392
  4.8 0.0 copy-start.2
  4.8 0.9 %copy-done.2 = f32[16,16,128]{2,1,0:T(8,128)S(1)} copy-done((f32[16,16,128]{2,1,0:T(8,128)S(1)}, f32[16,16,128]{2,1,0:T(8,128)}, u32[]{:S(2)}) %copy-start.2) | copy-done | bytes 131096
  5.7 0.0 copy-start.3
  5.7 0.9 %copy-done.3 = s32[16,16,128]{2,1,0:T(8,128)S(1)} copy-done((s32[16,16,128]{2,1,0:T(8,128)S(1)}, s32[16,16,128]{2,1,0:T(8,128)}, u32[]{:S(2)}) %copy-start.3) | copy-done | bytes 131096
  6.6 0.0 copy-start.4
  6.6 0.9 %copy-done.4 = s32[16,16,128]{2,1,0:T(8,128)S(1)} copy-done((s32[16,16,128]{2,1,0:T(8,128)S(1)}, s32[16,16,128]{2,1,0:T(8,128)}, u32[]{:S(2)}) %copy-start.4) | copy-done | bytes 131096
  7.5 26.4 %shard_map.86 = (f32[19,256,128]{2,1,0:T(8,128)S(1)}, f32[1,256]{1,0:T(1,128)S(1)}) custom-call(f32[19,256,128]{2,1,0:T(8,128)S(1)} %bitcast.13, f32[256,128]{1,0:T(8,128)S(1)} %bitcast.16, f32[19,256,128]{2,1,0:T(8,128)S(1)} %bitcast.14, s32[256,128]{1,0:T(8,128)S(1)} %bitcast.17, s32[256,128]{1,0:T(8,128)S(1)} %bitcast.18, f32[1,128]{1,0:T(1,128)S(1)} %concatenate.3.ids_ref), custom_call_target="tpu_custom_call" | custom-call | tf_op jit(solution)/shard_map/pallas_call | solution.py:420
  33.9 1.5 %copy.11 = f32[19,16,16,128]{3,2,1,0:T(8,128)} copy(f32[19,16,16,128]{3,2,1,0:T(8,128)S(1)} %bitcast.15) | data formatting | bytes 4980736
  35.3 0.6 %copy.12 = f32[256]{0:T(256)} copy(f32[256]{0:T(256)S(1)} %bitcast.19) | data formatting | bytes 2048
Async XLA Ops:
  1.4 1.7 %copy-start = (f32[19,16,16,128]{3,2,1,0:T(8,128)S(1)}, f32[19,16,16,128]{3,2,1,0:T(8,128)}, u32[]{:S(2)}) copy-start(f32[19,16,16,128]{3,2,1,0:T(8,128)} %param.7) | copy-start | bytes 7471108
  3.1 1.7 %copy-start.1 = (f32[19,16,16,128]{3,2,1,0:T(8,128)S(1)}, f32[19,16,16,128]{3,2,1,0:T(8,128)}, u32[]{:S(2)}) copy-start(f32[19,16,16,128]{3,2,1,0:T(8,128)} %param.9) | copy-start | bytes 7471108
  4.8 0.9 %copy-start.2 = (f32[16,16,128]{2,1,0:T(8,128)S(1)}, f32[16,16,128]{2,1,0:T(8,128)}, u32[]{:S(2)}) copy-start(f32[16,16,128]{2,1,0:T(8,128)} %param.8) | copy-start | bytes 393220
  5.7 0.9 %copy-start.3 = (s32[16,16,128]{2,1,0:T(8,128)S(1)}, s32[16,16,128]{2,1,0:T(8,128)}, u32[]{:S(2)}) copy-start(s32[16,16,128]{2,1,0:T(8,128)} %param.10) | copy-start | bytes 393220
  6.6 0.9 %copy-start.4 = (s32[16,16,128]{2,1,0:T(8,128)S(1)}, s32[16,16,128]{2,1,0:T(8,128)}, u32[]{:S(2)}) copy-start(s32[16,16,128]{2,1,0:T(8,128)} %param.11) | copy-start | bytes 393220
where the time goes:
time: 36.2 us; the launch traced here: 35.9 us
  Pallas kernels  26.4 us (73%)
  local copies, waits for them, and re-layouts  8.2 us (23%)
  other arithmetic  0.68 us (2%)
  between operations  0.64 us (2%)
    pallas_call x1, Pallas kernels, body(): pl.pallas_call(partial(kernel, (*sizes, cx, cy, nz)), out_shape=(jax.Shap...  26.4 us
    unnamed x12, local copies, waits for them, and re-layouts  8.13 us

commit v1 on v0

--- a/solution.py
+++ b/solution.py
@@ -63,7 +63,7 @@
 
 
 def forward(f, phi):
-    _, _, _, (second, product, first, other, fourth) = nonequilibrium(f)
+    _, _, u, (second, product, first, other, fourth) = nonequilibrium(f)
     second = [v * (0.5 * RATE2) for v in second]
     product = [v * (0.25 * RATE2) for v in product]
     first = [v * (0.25 * RATE3) for v in first]
@@ -90,11 +90,11 @@
         change[start : start + 4] = [h + p, h - p, k + q, k - q]
     relaxed = [f[i] - change[i] for i in range(19)]
     opposite = [0] + [i + 1 if i % 2 else i - 1 for i in range(1, 19)]
-    return [relaxed[i] + phi * (f[opposite[i]] - relaxed[i]) for i in range(19)]
-
-
-def backward(f, a, phi):
-    f_planes, f_diffs, (ux, uy, uz), moments = nonequilibrium(f)
+    gap = [f[opposite[i]] - relaxed[i] for i in range(19)]
+    return [relaxed[i] + phi * gap[i] for i in range(19)], gap, u
+
+
+def adjoint_moments(a):
     a_planes = split_planes(a)
     a_sums, a_diffs = split_faces(a)
     half = [0.5 * v for v in a_sums]
@@ -113,15 +113,26 @@
         RATE4 * (0.25 * n_xz[0] - (half[0] + half[2]) + a[0]),
         RATE4 * (0.25 * n_yz[0] - (half[1] + half[2]) + a[0]),
     ]
-    sens = None
-    for mine, theirs in zip((b2, b11, b_first, b_other, b4), moments):
+    return a_planes, a_diffs, (b2, b11, b_first, b_other, b4)
+
+
+def fraction_cotangent(f_planes, f_diffs, moments, a_planes, a_diffs, b):
+    parts = []
+    for mine, theirs in zip(b, moments):
+        part = None
         for v, m in zip(mine, theirs):
-            sens = v * m if sens is None else sens + v * m
+            part = v * m if part is None else part + v * m
+        parts.append(part)
     for axis in range(3):
-        sens = sens - f_diffs[axis] * a_diffs[axis]
-    for p, n in zip(f_planes, a_planes):
-        sens = sens - p[4] * n[4] - p[5] * n[5]
-
+        parts[axis] = parts[axis] - f_diffs[axis] * a_diffs[axis]
+    for k, (p, n) in enumerate(zip(f_planes, a_planes)):
+        parts[k + 2] = parts[k + 2] - p[4] * n[4] - p[5] * n[5]
+    return ((parts[0] + parts[1]) + (parts[2] + parts[3])) + parts[4]
+
+
+def population_cotangent(u, a, b, phi):
+    ux, uy, uz = u
+    b2, b11, b_first, b_other, b4 = b
     keep = 1.0 - phi
     b2, b11, b_first, b_other, b4 = [
         [keep * v for v in part] for part in (b2, b11, b_first, b_other, b4)
@@ -144,7 +155,7 @@
     result[0] = a[0] - r0
     evens = [r0 + b2[0], r0 + b2[1], r0 + b2[2]]
     for axis, odd in enumerate((rx, ry, rz)):
-        back = phi * a_diffs[axis] + odd
+        back = phi * (a[1 + 2 * axis] - a[2 + 2 * axis]) + odd
         result[1 + 2 * axis] = (a[1 + 2 * axis] - evens[axis]) - back
         result[2 + 2 * axis] = (a[2 + 2 * axis] - evens[axis]) + back
     for plane, (start, one, two) in enumerate(((7, 0, 1), (11, 0, 2), (15, 1, 2))):
@@ -152,20 +163,21 @@
         p = (rx, ry, rz)[one] + b_first[plane]
         q = (rx, ry, rz)[two] + b_other[plane]
         h, k = even + b11[plane], even - b11[plane]
-        s = (p + q) + phi * a_planes[plane][4]
-        t = (p - q) + phi * a_planes[plane][5]
+        s = (p + q) + phi * (a[start] - a[start + 1])
+        t = (p - q) + phi * (a[start + 2] - a[start + 3])
         result[start] = (a[start] - h) - s
         result[start + 1] = (a[start + 1] - h) + s
         result[start + 2] = (a[start + 2] - k) - t
         result[start + 3] = (a[start + 3] - k) + t
-    return result, sens
+    return result
 
 
 def kernel(
-    sizes, pops_hbm, porosity_hbm, adj_hbm, porous_hbm, walls_hbm, ids_ref, out_hbm, patch_ref,
-    pops, porosity, adj, porous, walls, out, ahead, behind, late_sens, early_sens,
-    y_send, y_recv, c_send, c_recv, message, gathered,
-    load_sem, store_sem, halo_send, halo_recv, patch_send, patch_recv,
+    sizes, pops_hbm, porosity_hbm, adj_hbm, porous_hbm, walls_hbm, owners_hbm, slots_hbm,
+    out, gathered,
+    pops, porosity, adj, porous, walls, owners, slots, gap, speed, ahead, behind,
+    late_sens, early_sens, y_send, y_recv, c_send, c_recv, message, names,
+    load_sem, halo_send, halo_recv, patch_send, patch_recv,
 ):
     n_gx, n_gy, cx, cy, nz = sizes
     n = n_gx * n_gy
@@ -173,12 +185,13 @@
     gx, gy = lax.axis_index("gx"), lax.axis_index("gy")
     me = gx * n_gy + gy
 
+    faces = [pl.ds(0, cy), pl.ds((cx - 1) * cy, cy)]
+    middle = pl.ds(cy, (cx - 2) * cy)
+    pairs = [(porosity_hbm, porosity), (porous_hbm, porous), (walls_hbm, walls)]
+    pairs += [(pops_hbm.at[:, part, :], pops.at[:, part, :]) for part in faces + [middle]]
+    pairs += [(adj_hbm, adj), (owners_hbm, owners), (slots_hbm, slots)]
     loads = [
-        pltpu.make_async_copy(src, dst, load_sem.at[k])
-        for k, (src, dst) in enumerate((
-            (porosity_hbm, porosity), (porous_hbm, porous), (walls_hbm, walls),
-            (pops_hbm, pops), (adj_hbm, adj),
-        ))
+        pltpu.make_async_copy(src, dst, load_sem.at[k]) for k, (src, dst) in enumerate(pairs)
     ]
     for load in loads:
         load.start()
@@ -232,35 +245,56 @@
         rows = window(x, y, along_x)
         f = [pops[i, rows, :] for i in range(19)]
         phi, _ = fractions(rows)
-        values = [spin(v, VELOCITIES[i][2]) for i, v in enumerate(forward(f, phi))]
+        values, apart, u = forward(f, phi)
+        values = [spin(v, VELOCITIES[i][2]) for i, v in enumerate(values)]
         if along_x:
             pack(0, values, x, y, 1)
         else:
             for i in range(19):
                 ahead[POS[i], padded(x, y, False), :] = values[i]
+                gap[i, rows, :] = apart[i]
+            for axis in range(3):
+                speed[axis, rows, :] = u[axis]
 
     def step_two(x, y, along_x):
         rows = window(x, y, along_x)
         f = [ahead[POS[i], shifted(x, y, i, 1, along_x), :] for i in range(19)]
-        a = [adj[i, rows, :] for i in range(19)]
         phi, weight = fractions(rows)
-        values, sens = backward(f, a, phi)
+        f_planes, f_diffs, u, moments = nonequilibrium(f)
+        a_planes, a_diffs, b = adjoint_moments([adj[i, rows, :] for i in range(19)])
+        sens = fraction_cotangent(f_planes, f_diffs, moments, a_planes, a_diffs, b)
+        late_sens[rows, :] = weight * sens
+        values = population_cotangent(u, [adj[i, rows, :] for i in range(19)], b, phi)
         values = [spin(v, -VELOCITIES[i][2]) for i, v in enumerate(values)]
-        late_sens[rows, :] = weight * sens
         if along_x:
             pack(1, values, x, y, -1)
         for i in range(19):
             behind[POS[i], padded(x, y, along_x), :] = values[i]
 
-    def step_three(x, y, along_x):
+    def pulled(x, y, along_x):
+        return [behind[POS[i], shifted(x, y, i, -1, along_x), :] for i in range(19)]
+
+    def step_sens(x, y, along_x):
         rows = window(x, y, along_x)
-        f = [pops[i, rows, :] for i in range(19)]
-        a = [behind[POS[i], shifted(x, y, i, -1, along_x), :] for i in range(19)]
-        phi, weight = fractions(rows)
-        values, sens = backward(f, a, phi)
-        early_sens[rows, :] = weight * sens
+        a = pulled(x, y, along_x)
+        parts = [a[i] * gap[i, rows, :] for i in range(4)]
+        for i in range(4, 19):
+            parts[i % 4] = parts[i % 4] + a[i] * gap[i, rows, :]
+        _, weight = fractions(rows)
+        early_sens[rows, :] = weight * ((parts[0] + parts[1]) + (parts[2] + parts[3]))
+
+    def step_out(x, y, along_x):
+        rows = window(x, y, along_x)
+        phi, _ = fractions(rows)
+        _, _, b = adjoint_moments(pulled(x, y, along_x))
+        u = [speed[axis, rows, :] for axis in range(3)]
+        values = population_cotangent(u, pulled(x, y, along_x), b, phi)
         for i in range(19):
             out[i, rows, :] = values[i]
+
+    def step_three(x, y, along_x):
+        step_sens(x, y, along_x)
+        step_out(x, y, along_x)
 
     def y_edges(step):
         for y in (0, cy - 1):
@@ -272,8 +306,8 @@
             for y in range(0, cy, 8):
                 step(x, y, False)
 
-    def inner(step):
-        @pl.loop(1, cx - 1)
+    def inner(step, start, stop):
+        @pl.loop(start, stop)
         def _(x):
             for y in range(0, cy, 8):
                 step(x, y, False)
@@ -325,28 +359,32 @@
             row = (0 if sx > 0 else cx + 1) * stride + 8 + (-1 if sy > 0 else cy)
             buffer[POS[i], pl.ds(row, 1), :] = c_recv[stage, number]
 
-    for load in loads[:4]:
+    names[...] = jnp.zeros_like(names)
+    for load in loads[:5]:
         load.wait()
+    x_faces(step_one)
+    pl.semaphore_wait(barrier, n - 1)
+    copies = send_x(0, ahead, 1)
+    loads[5].wait()
     y_edges(step_one)
-    pl.semaphore_wait(barrier, n - 1)
-    copies = send_y(0)
-    x_faces(step_one)
-    copies += send_x(0, ahead, 1)
-    inner(step_one)
-    loads[4].wait()
-    inner(step_two)
+    copies += send_y(0)
+    inner(step_one, 1, cx - 1)
+    for load in loads[6:]:
+        load.wait()
+    names[pl.ds(0, 1), pl.ds(0, owners.shape[1])] = (
+        owners[...] * PATCH_DEV + slots[...]
+    ).astype(jnp.float32)
+    inner(step_two, 1, cx // 2)
     receive(0, copies, ahead, 1)
     y_edges(step_two)
     later = send_y(1)
     x_faces(step_two)
     later += send_x(1, behind, -1)
-    inner(step_three)
+    inner(step_two, cx // 2, cx - 1)
+    inner(step_three, 1, cx - 1)
     receive(1, later, behind, -1)
-    y_edges(step_three)
-    x_faces(step_three)
-
-    store = pltpu.make_async_copy(out, out_hbm, store_sem)
-    store.start()
+    y_edges(step_sens)
+    x_faces(step_sens)
 
     rows_of = []
     for x in range(0, cx, 2):
@@ -364,7 +402,7 @@
         ones, jnp.concatenate(rows_of, axis=0), contract,
         precision=lax.Precision.HIGHEST, preferred_element_type=jnp.float32,
     )
-    note = sums[0:1, :] + ids_ref[...]
+    note = sums[0:1, :] + pltpu.roll(names[...], nz // 2, 1)[0:1, :]
     message[0] = note
     gathered[0] = note
 
@@ -379,11 +417,22 @@
     def _(k):
         patch_copy(k).start()
 
+    y_edges(step_out)
+    x_faces(step_out)
+
     for copy in copies + later:
         copy.wait_send()
     others = gathered.at[pl.ds(1, n - 1)]
     pltpu.make_async_copy(others, others, patch_recv).wait()
-
+    pltpu.make_async_copy(others, others, patch_send).wait()
+
+
+def finish(sizes, result, gathered, out_hbm, patch_ref, store_sem):
+    n_gx, n_gy, _, _, nz = sizes
+    n = n_gx * n_gy
+    store = pltpu.make_async_copy(result, out_hbm, store_sem)
+    store.start()
+    me = lax.axis_index("gx") * n_gy + lax.axis_index("gy")
     lane = lax.broadcasted_iota(jnp.int32, (1, nz), 1)
     low = lane < nz // 2
     patch = lax.broadcasted_iota(jnp.int32, (PATCH_DEV, nz), 0).astype(jnp.float32)
@@ -398,11 +447,10 @@
 
     total = lax.fori_loop(0, n // 2, add, jnp.zeros((PATCH_DEV, nz), jnp.float32))
     summed = lax.dot_general(
-        ones, total, contract,
+        jnp.ones((8, nz), jnp.float32), total, (((1,), (1,)), ((), ())),
         precision=lax.Precision.HIGHEST, preferred_element_type=jnp.float32,
     )
     patch_ref[...] = summed[0:1, :]
-    pltpu.make_async_copy(others, others, patch_send).wait()
     store.wait()
 
 
@@ -410,27 +458,30 @@
     _, cx, cy, nz = populations.shape
     rows = cx * cy
     n = sizes[0] * sizes[1]
-    ids = (owners.reshape(1, -1) * PATCH_DEV + slots.reshape(1, -1)).astype(jnp.float32)
-    ids = jnp.concatenate([jnp.zeros((1, nz - ids.shape[1]), jnp.float32), ids], axis=1)
     flat = lambda v: v.reshape(v.shape[:-3] + (rows, nz))
-    anywhere = pl.BlockSpec(memory_space=pl.ANY)
+    row = lambda v: v.reshape(1, -1)
+    hbm = pl.BlockSpec(memory_space=pltpu.HBM)
     vmem = pl.BlockSpec(memory_space=pltpu.VMEM)
     wide = (19, (cx + 2) * (cy + 16), nz)
     f32 = jnp.float32
-    result, patch = pl.pallas_call(
-        partial(kernel, (*sizes, cx, cy, nz)),
-        out_shape=(
-            jax.ShapeDtypeStruct((19, rows, nz), f32), jax.ShapeDtypeStruct((1, PATCH_DEV), f32)
-        ),
-        in_specs=[anywhere] * 5 + [vmem],
-        out_specs=(anywhere, vmem),
+    whole = jax.ShapeDtypeStruct((19, rows, nz), f32)
+    shape = (*sizes, cx, cy, nz)
+    blocks = slots.shape[-1]
+    result, gathered = pl.pallas_call(
+        partial(kernel, shape),
+        out_shape=(whole, jax.ShapeDtypeStruct((n, 1, nz), f32)),
+        in_specs=[hbm] * 7,
+        out_specs=(vmem, vmem),
         scratch_shapes=[
             pltpu.VMEM((19, rows, nz), f32),
             pltpu.VMEM((rows, nz), f32),
             pltpu.VMEM((19, rows, nz), f32),
             pltpu.VMEM((rows, nz), jnp.int32),
             pltpu.VMEM((rows, nz), jnp.int32),
+            pltpu.VMEM((1, blocks), jnp.int32),
+            pltpu.VMEM((1, blocks), jnp.int32),
             pltpu.VMEM((19, rows, nz), f32),
+            pltpu.VMEM((3, rows, nz), f32),
             pltpu.VMEM(wide, f32),
             pltpu.VMEM(wide, f32),
             pltpu.VMEM((rows, nz), f32),
@@ -440,9 +491,8 @@
             pltpu.VMEM((2, 4, 1, nz), f32),
             pltpu.VMEM((2, 4, 1, nz), f32),
             pltpu.VMEM((1, 1, nz), f32),
-            pltpu.VMEM((n, 1, nz), f32),
-            pltpu.SemaphoreType.DMA((5,)),
-            pltpu.SemaphoreType.DMA,
+            pltpu.VMEM((8, nz), f32),
+            pltpu.SemaphoreType.DMA((9,)),
             pltpu.SemaphoreType.DMA((2, 8)),
             pltpu.SemaphoreType.DMA((2, 8)),
             pltpu.SemaphoreType.DMA,
@@ -451,8 +501,19 @@
         compiler_params=pltpu.CompilerParams(
             collective_id=0, has_side_effects=True, vmem_limit_bytes=40 * 1024 * 1024
         ),
-    )(flat(populations), flat(porosity), flat(adjoint_in), flat(porous), flat(walls), ids)
-    return result.reshape(populations.shape), patch.reshape(-1)
+    )(
+        *[pltpu.with_memory_space_constraint(v, pltpu.HBM) for v in (flat(populations), flat(porosity), flat(adjoint_in), flat(porous), flat(walls),
+        row(owners), row(slots))],
+    )
+    adjoint_out, patch = pl.pallas_call(
+        partial(finish, shape),
+        out_shape=(whole, jax.ShapeDtypeStruct((1, PATCH_DEV), f32)),
+        in_specs=[vmem, vmem],
+        out_specs=(hbm, vmem),
+        scratch_shapes=[pltpu.SemaphoreType.DMA],
+        compiler_params=pltpu.CompilerParams(vmem_limit_bytes=16 * 1024 * 1024),
+    )(result, gathered)
+    return adjoint_out.reshape(populations.shape), patch.reshape(-1)
 
 
 def solution(mesh):

time: 36.2 us -> 24.6 us (0.68)
  local copies, waits for them, and re-layouts: 8.2 us -> 0 us
  Pallas kernels: 26.4 us -> 23.8 us
  other arithmetic: 0.68 us -> 0 us
    unnamed x12 -> x0, local copies, waits for them, and re-layouts: 8.13 us -> none
    pallas_call x1 -> x2, Pallas kernels: 26.4 us -> 23.8 us  [the longest x1 21.5 us: body(): pl.pallas_call(partial(kernel, shape), out_shape=(whole, jax.ShapeDtypeSt...]
    convert_element_type x1 -> x0, other arithmetic: 0.68 us -> none  [body(): (owners.reshape(1, -1) * PATCH_DEV + slots.reshape(1, -1)).astype(jnp.flo...]
where the time goes in v1:
time: 24.6 us; the launch traced here: 24.5 us
  Pallas kernels  23.8 us (97%)
  between operations  0.64 us (3%)
    pallas_call x1, Pallas kernels, body(): pl.pallas_call(partial(kernel, shape), out_shape=(whole, jax.ShapeDtypeSt...  21.5 us
    pallas_call x1, Pallas kernels, body(): pl.pallas_call(partial(finish, shape), out_shape=(whole, jax.ShapeDtypeSt...  2.35 us

profile of v1, /device:TPU:0, one launch (start us, length us, event | category | flops | bytes accessed | tf_op | source)
XLA Modules:
  0.0 24.5 jit_solution(14826149232390504696)
XLA Ops:
  0.6 21.5 %shard_map.86 = (f32[19,256,128]{2,1,0:T(8,128)S(1)}, f32[32,1,128]{2,1,0:T(1,128)S(1)}) custom-call(f32[19,256,128]{2,1,0:T(8,128)} %bitcast.9, f32[256,128]{1,0:T(8,128)} %bitcast.11, f32[19,256,128]{2,1,0:T(8,128)} %bitcast.10, s32[256,128]{1,0:T(8,128)} %bitcast.12, s32[256,128]{1,0:T(8,128)} %bitcast.13, s32[1,64]{1,0:T(1,128)} %bitcast.14, ...), custom_call_target="tpu_custom_call" | custom-call | tf_op jit(solution)/shard_map/pallas_call | solution.py:470
  22.1 2.3 %shard_map.87 = (f32[19,256,128]{2,1,0:T(8,128)}, f32[1,256]{1,0:T(1,128)}) custom-call(f32[19,256,128]{2,1,0:T(8,128)S(1)} %get-tuple-element.6.result, f32[32,1,128]{2,1,0:T(1,128)S(1)} %get-tuple-element.7.gathered), custom_call_target="tpu_custom_call" | custom-call | tf_op jit(solution)/shard_map/pallas_call | solution.py:508

commit v2 on v1

--- a/solution.py
+++ b/solution.py
@@ -1,3 +1,4 @@
+from collections import namedtuple
 from functools import partial
 
 import jax
@@ -25,6 +26,12 @@
 CORNER_POP = {(1, 1): 7, (-1, -1): 8, (1, -1): 9, (-1, 1): 10}
 PLANES = (7, 11, 15)
 RATE2, RATE3, RATE4 = 1.25, 1.5, 1.4
+
+
+Node = namedtuple("Node", [
+    "pops", "porosity", "adj", "porous", "walls", "out", "gap", "speed", "late_sens", "early_sens",
+    "ahead", "behind",
+])
 
 
 def split_planes(f):
@@ -224,10 +231,22 @@
         row = (x + 1) * stride + 8 + y
         return pl.ds(row, 8, stride=stride) if along_x else pl.ds(row, 8)
 
-    def fractions(rows):
-        porous_here = porous[rows, :].astype(jnp.float32)
-        wall = walls[rows, :] == 1
-        phi = jnp.where(wall, 1.0, porous_here * porosity[rows, :])
+    whole = Node(
+        pops, porosity, adj, porous, walls, out, gap, speed, late_sens, early_sens, ahead, behind
+    )
+
+    def layer(x):
+        plain = pl.ds(pl.multiple_of(x * cy, cy), cy)
+        wide = pl.ds(pl.multiple_of(x * stride, stride), 3 * stride)
+        parts = [
+            ref.at[plain, :] if len(ref.shape) == 2 else ref.at[:, plain, :] for ref in whole[:10]
+        ]
+        return Node(*parts, ahead.at[:, wide, :], behind.at[:, wide, :])
+
+    def fractions(node, rows):
+        porous_here = node.porous[rows, :].astype(jnp.float32)
+        wall = node.walls[rows, :] == 1
+        phi = jnp.where(wall, 1.0, porous_here * node.porosity[rows, :])
         return phi, jnp.where(wall, 0.0, porous_here)
 
     def pack(stage, values, x, y, sign):
@@ -241,76 +260,73 @@
                 row = 7 if sx > 0 else 0
                 c_send[stage, number, :, :] = value[row : row + 1, :]
 
-    def step_one(x, y, along_x):
+    def step_one(node, x, y, along_x):
         rows = window(x, y, along_x)
-        f = [pops[i, rows, :] for i in range(19)]
-        phi, _ = fractions(rows)
+        f = [node.pops[i, rows, :] for i in range(19)]
+        phi, _ = fractions(node, rows)
         values, apart, u = forward(f, phi)
         values = [spin(v, VELOCITIES[i][2]) for i, v in enumerate(values)]
         if along_x:
             pack(0, values, x, y, 1)
         else:
             for i in range(19):
-                ahead[POS[i], padded(x, y, False), :] = values[i]
-                gap[i, rows, :] = apart[i]
+                node.ahead[POS[i], padded(x, y, False), :] = values[i]
+                node.gap[i, rows, :] = apart[i]
             for axis in range(3):
-                speed[axis, rows, :] = u[axis]
-
-    def step_two(x, y, along_x):
+                node.speed[axis, rows, :] = u[axis]
+
+    def step_two(node, x, y, along_x):
         rows = window(x, y, along_x)
-        f = [ahead[POS[i], shifted(x, y, i, 1, along_x), :] for i in range(19)]
-        phi, weight = fractions(rows)
+        f = [node.ahead[POS[i], shifted(x, y, i, 1, along_x), :] for i in range(19)]
+        phi, weight = fractions(node, rows)
         f_planes, f_diffs, u, moments = nonequilibrium(f)
-        a_planes, a_diffs, b = adjoint_moments([adj[i, rows, :] for i in range(19)])
+        a_planes, a_diffs, b = adjoint_moments([node.adj[i, rows, :] for i in range(19)])
         sens = fraction_cotangent(f_planes, f_diffs, moments, a_planes, a_diffs, b)
-        late_sens[rows, :] = weight * sens
-        values = population_cotangent(u, [adj[i, rows, :] for i in range(19)], b, phi)
+        node.late_sens[rows, :] = weight * sens
+        values = population_cotangent(u, [node.adj[i, rows, :] for i in range(19)], b, phi)
         values = [spin(v, -VELOCITIES[i][2]) for i, v in enumerate(values)]
         if along_x:
             pack(1, values, x, y, -1)
         for i in range(19):
-            behind[POS[i], padded(x, y, along_x), :] = values[i]
-
-    def pulled(x, y, along_x):
-        return [behind[POS[i], shifted(x, y, i, -1, along_x), :] for i in range(19)]
-
-    def step_sens(x, y, along_x):
+            node.behind[POS[i], padded(x, y, along_x), :] = values[i]
+
+    def pulled(node, x, y, along_x):
+        return [node.behind[POS[i], shifted(x, y, i, -1, along_x), :] for i in range(19)]
+
+    def step_sens(node, x, y, along_x):
         rows = window(x, y, along_x)
-        a = pulled(x, y, along_x)
-        parts = [a[i] * gap[i, rows, :] for i in range(4)]
+        a = pulled(node, x, y, along_x)
+        parts = [a[i] * node.gap[i, rows, :] for i in range(4)]
         for i in range(4, 19):
-            parts[i % 4] = parts[i % 4] + a[i] * gap[i, rows, :]
-        _, weight = fractions(rows)
-        early_sens[rows, :] = weight * ((parts[0] + parts[1]) + (parts[2] + parts[3]))
-
-    def step_out(x, y, along_x):
+            parts[i % 4] = parts[i % 4] + a[i] * node.gap[i, rows, :]
+        _, weight = fractions(node, rows)
+        node.early_sens[rows, :] = weight * ((parts[0] + parts[1]) + (parts[2] + parts[3]))
+
+    def step_out(node, x, y, along_x):
         rows = window(x, y, along_x)
-        phi, _ = fractions(rows)
-        _, _, b = adjoint_moments(pulled(x, y, along_x))
-        u = [speed[axis, rows, :] for axis in range(3)]
-        values = population_cotangent(u, pulled(x, y, along_x), b, phi)
+        phi, _ = fractions(node, rows)
+        _, _, b = adjoint_moments(pulled(node, x, y, along_x))
+        u = [node.speed[axis, rows, :] for axis in range(3)]
+        values = population_cotangent(u, pulled(node, x, y, along_x), b, phi)
         for i in range(19):
-            out[i, rows, :] = values[i]
-
-    def step_three(x, y, along_x):
-        step_sens(x, y, along_x)
-        step_out(x, y, along_x)
-
-    def y_edges(step):
+            node.out[i, rows, :] = values[i]
+
+    def y_edges(step, stop):
         for y in (0, cy - 1):
-            for x in range(0, cx, 8):
-                step(x, y, True)
+            for x in range(0, stop, 8):
+                step(whole, x, y, True)
 
     def x_faces(step):
         for x in (0, cx - 1):
             for y in range(0, cy, 8):
-                step(x, y, False)
+                step(whole, x, y, False)
 
     def inner(step, start, stop):
         @pl.loop(start, stop)
         def _(x):
+            node = layer(x)
             for y in range(0, cy, 8):
-                step(x, y, False)
+                step(node, 0, y, False)
 
     def send(stage, number, src, dst, dx, dy):
         copy = pltpu.make_async_remote_copy(
@@ -366,7 +382,7 @@
     pl.semaphore_wait(barrier, n - 1)
     copies = send_x(0, ahead, 1)
     loads[5].wait()
-    y_edges(step_one)
+    y_edges(step_one, cx)
     copies += send_y(0)
     inner(step_one, 1, cx - 1)
     for load in loads[6:]:
@@ -376,14 +392,15 @@
     ).astype(jnp.float32)
     inner(step_two, 1, cx // 2)
     receive(0, copies, ahead, 1)
-    y_edges(step_two)
+    y_edges(step_two, cx)
     later = send_y(1)
     x_faces(step_two)
     later += send_x(1, behind, -1)
     inner(step_two, cx // 2, cx - 1)
-    inner(step_three, 1, cx - 1)
+    inner(step_sens, 1, cx - 1)
+    inner(step_out, 1, cx // 2)
     receive(1, later, behind, -1)
-    y_edges(step_sens)
+    y_edges(step_sens, cx)
     x_faces(step_sens)
 
     rows_of = []
@@ -417,8 +434,9 @@
     def _(k):
         patch_copy(k).start()
 
-    y_edges(step_out)
+    y_edges(step_out, cx // 2)
     x_faces(step_out)
+    inner(step_out, cx // 2, cx - 1)
 
     for copy in copies + later:
         copy.wait_send()
@@ -427,11 +445,16 @@
     pltpu.make_async_copy(others, others, patch_send).wait()
 
 
-def finish(sizes, result, gathered, out_hbm, patch_ref, store_sem):
+def finish(sizes, result, gathered, out_hbm, patch_hbm, patch_ref, store_sem):
     n_gx, n_gy, _, _, nz = sizes
     n = n_gx * n_gy
-    store = pltpu.make_async_copy(result, out_hbm, store_sem)
-    store.start()
+    parts = [pl.ds(0, 10), pl.ds(10, 9)]
+    stores = [
+        pltpu.make_async_copy(result.at[part], out_hbm.at[part], store_sem.at[k])
+        for k, part in enumerate(parts)
+    ]
+    for store in stores:
+        store.start()
     me = lax.axis_index("gx") * n_gy + lax.axis_index("gy")
     lane = lax.broadcasted_iota(jnp.int32, (1, nz), 1)
     low = lane < nz // 2
@@ -451,7 +474,10 @@
         precision=lax.Precision.HIGHEST, preferred_element_type=jnp.float32,
     )
     patch_ref[...] = summed[0:1, :]
-    store.wait()
+    stores.append(pltpu.make_async_copy(patch_ref, patch_hbm, store_sem.at[2]))
+    stores[-1].start()
+    for store in stores:
+        store.wait()
 
 
 def body(sizes, populations, porosity, adjoint_in, porous, walls, owners, slots):
@@ -467,6 +493,8 @@
     whole = jax.ShapeDtypeStruct((19, rows, nz), f32)
     shape = (*sizes, cx, cy, nz)
     blocks = slots.shape[-1]
+    arguments = [flat(v) for v in (populations, porosity, adjoint_in, porous, walls)]
+    arguments += [row(owners), row(slots)]
     result, gathered = pl.pallas_call(
         partial(kernel, shape),
         out_shape=(whole, jax.ShapeDtypeStruct((n, 1, nz), f32)),
@@ -502,15 +530,14 @@
             collective_id=0, has_side_effects=True, vmem_limit_bytes=40 * 1024 * 1024
         ),
     )(
-        *[pltpu.with_memory_space_constraint(v, pltpu.HBM) for v in (flat(populations), flat(porosity), flat(adjoint_in), flat(porous), flat(walls),
-        row(owners), row(slots))],
+        *[pltpu.with_memory_space_constraint(v, pltpu.HBM) for v in arguments]
     )
     adjoint_out, patch = pl.pallas_call(
         partial(finish, shape),
         out_shape=(whole, jax.ShapeDtypeStruct((1, PATCH_DEV), f32)),
         in_specs=[vmem, vmem],
-        out_specs=(hbm, vmem),
-        scratch_shapes=[pltpu.SemaphoreType.DMA],
+        out_specs=(hbm, hbm),
+        scratch_shapes=[pltpu.VMEM((1, PATCH_DEV), f32), pltpu.SemaphoreType.DMA((3,))],
         compiler_params=pltpu.CompilerParams(vmem_limit_bytes=16 * 1024 * 1024),
     )(result, gathered)
     return adjoint_out.reshape(populations.shape), patch.reshape(-1)

time: 24.6 us -> 24.6 us (level)
  no operation moved by 1% of the time
where the time goes in v2:
time: 24.6 us; the launch traced here: 24.5 us
  Pallas kernels  23.8 us (97%)
  between operations  0.64 us (3%)
    pallas_call x1, Pallas kernels, body(): pl.pallas_call(partial(kernel, shape), out_shape=(whole, jax.ShapeDtypeSt...  21.5 us
    pallas_call x1, Pallas kernels, body(): pl.pallas_call(partial(finish, shape), out_shape=(whole, jax.ShapeDtypeSt...  2.37 us

profile of v2, /device:TPU:0, one launch (start us, length us, event | category | flops | bytes accessed | tf_op | source)
XLA Modules:
  0.0 24.5 jit_solution(15077894258243524838)
XLA Ops:
  0.6 21.5 %shard_map.86 = (f32[19,256,128]{2,1,0:T(8,128)S(1)}, f32[32,1,128]{2,1,0:T(1,128)S(1)}) custom-call(f32[19,256,128]{2,1,0:T(8,128)} %bitcast.9, f32[256,128]{1,0:T(8,128)} %bitcast.11, f32[19,256,128]{2,1,0:T(8,128)} %bitcast.10, s32[256,128]{1,0:T(8,128)} %bitcast.12, s32[256,128]{1,0:T(8,128)} %bitcast.13, s32[1,64]{1,0:T(1,128)} %bitcast.14, ...), custom_call_target="tpu_custom_call" | custom-call | tf_op jit(solution)/shard_map/pallas_call | solution.py:498
  22.1 2.4 %shard_map.87 = (f32[19,256,128]{2,1,0:T(8,128)}, f32[1,256]{1,0:T(1,128)}) custom-call(f32[19,256,128]{2,1,0:T(8,128)S(1)} %get-tuple-element.6.result, f32[32,1,128]{2,1,0:T(1,128)S(1)} %get-tuple-element.7.gathered), custom_call_target="tpu_custom_call" | custom-call | tf_op jit(solution)/shard_map/pallas_call | solution.py:535

commit v3 on v2

--- a/solution.py
+++ b/solution.py
@@ -190,7 +190,6 @@
     n = n_gx * n_gy
     stride = cy + 16
     gx, gy = lax.axis_index("gx"), lax.axis_index("gy")
-    me = gx * n_gy + gy
 
     faces = [pl.ds(0, cy), pl.ds((cx - 1) * cy, cy)]
     middle = pl.ds(cy, (cx - 2) * cy)
@@ -203,18 +202,26 @@
     for load in loads:
         load.start()
 
-    def place(k):
-        index = lax.rem(me + k, n)
-        return (index // n_gy, lax.rem(index, n_gy))
+    def near(dx, dy):
+        x, y = gx + dx, gy + dy
+        return (
+            jnp.where(x >= n_gx, x - n_gx, jnp.where(x < 0, x + n_gx, x)),
+            jnp.where(y >= n_gy, y - n_gy, jnp.where(y < 0, y + n_gy, y)),
+        )
+
+    def for_others(act):
+        for dy in range(1, n_gy):
+            act(0, dy)
+
+        @pl.loop(1, n_gx)
+        def _(dx):
+            for dy in range(n_gy):
+                act(dx, dy)
 
     barrier = pltpu.get_barrier_semaphore()
-
-    @pl.loop(1, n)
-    def _(k):
-        pl.semaphore_signal(barrier, inc=1, device_id=place(k), device_id_type=MESH)
-
-    def near(dx, dy):
-        return (lax.rem(gx + (dx + n_gx), n_gx), lax.rem(gy + (dy + n_gy), n_gy))
+    for_others(lambda dx, dy: pl.semaphore_signal(
+        barrier, inc=1, device_id=near(dx, dy), device_id_type=MESH
+    ))
 
     def spin(value, shift):
         return value if shift == 0 else pltpu.roll(value, shift % nz, 1)
@@ -235,9 +242,9 @@
         pops, porosity, adj, porous, walls, out, gap, speed, late_sens, early_sens, ahead, behind
     )
 
-    def layer(x):
-        plain = pl.ds(pl.multiple_of(x * cy, cy), cy)
-        wide = pl.ds(pl.multiple_of(x * stride, stride), 3 * stride)
+    def layer(x, count):
+        plain = pl.ds(pl.multiple_of(x * cy, cy), count * cy)
+        wide = pl.ds(pl.multiple_of(x * stride, stride), (count + 2) * stride)
         parts = [
             ref.at[plain, :] if len(ref.shape) == 2 else ref.at[:, plain, :] for ref in whole[:10]
         ]
@@ -253,21 +260,16 @@
         side = 1 if y else -1
         which = 0 if side > 0 else 1
         for k, i in enumerate(Y_GROUP[side * sign]):
-            y_send[stage, which, k, pl.ds(x, 8), :] = values[i]
-        for number, (sx, sy) in enumerate(CORNERS):
-            if sy == side and x == (cx - 8 if sx > 0 else 0):
-                value = values[CORNER_POP[(sx * sign, sy * sign)]]
-                row = 7 if sx > 0 else 0
-                c_send[stage, number, :, :] = value[row : row + 1, :]
-
-    def step_one(node, x, y, along_x):
+            y_send[stage, which, k, pl.ds(pl.multiple_of(x, 8), 8), :] = values[i]
+
+    def step_one(node, x, y, along_x, at=0):
         rows = window(x, y, along_x)
         f = [node.pops[i, rows, :] for i in range(19)]
         phi, _ = fractions(node, rows)
         values, apart, u = forward(f, phi)
         values = [spin(v, VELOCITIES[i][2]) for i, v in enumerate(values)]
         if along_x:
-            pack(0, values, x, y, 1)
+            pack(0, values, at, y, 1)
         else:
             for i in range(19):
                 node.ahead[POS[i], padded(x, y, False), :] = values[i]
@@ -275,7 +277,7 @@
             for axis in range(3):
                 node.speed[axis, rows, :] = u[axis]
 
-    def step_two(node, x, y, along_x):
+    def step_two(node, x, y, along_x, at=0):
         rows = window(x, y, along_x)
         f = [node.ahead[POS[i], shifted(x, y, i, 1, along_x), :] for i in range(19)]
         phi, weight = fractions(node, rows)
@@ -286,14 +288,14 @@
         values = population_cotangent(u, [node.adj[i, rows, :] for i in range(19)], b, phi)
         values = [spin(v, -VELOCITIES[i][2]) for i, v in enumerate(values)]
         if along_x:
-            pack(1, values, x, y, -1)
+            pack(1, values, at, y, -1)
         for i in range(19):
             node.behind[POS[i], padded(x, y, along_x), :] = values[i]
 
     def pulled(node, x, y, along_x):
         return [node.behind[POS[i], shifted(x, y, i, -1, along_x), :] for i in range(19)]
 
-    def step_sens(node, x, y, along_x):
+    def step_sens(node, x, y, along_x, at=0):
         rows = window(x, y, along_x)
         a = pulled(node, x, y, along_x)
         parts = [a[i] * node.gap[i, rows, :] for i in range(4)]
@@ -302,7 +304,7 @@
         _, weight = fractions(node, rows)
         node.early_sens[rows, :] = weight * ((parts[0] + parts[1]) + (parts[2] + parts[3]))
 
-    def step_out(node, x, y, along_x):
+    def step_out(node, x, y, along_x, at=0):
         rows = window(x, y, along_x)
         phi, _ = fractions(node, rows)
         _, _, b = adjoint_moments(pulled(node, x, y, along_x))
@@ -313,8 +315,9 @@
 
     def y_edges(step, stop):
         for y in (0, cy - 1):
-            for x in range(0, stop, 8):
-                step(whole, x, y, True)
+            @pl.loop(0, stop // 8)
+            def _(part):
+                step(layer(part * 8, 8), 0, y, True, part * 8)
 
     def x_faces(step):
         for x in (0, cx - 1):
@@ -324,7 +327,7 @@
     def inner(step, start, stop):
         @pl.loop(start, stop)
         def _(x):
-            node = layer(x)
+            node = layer(x, 1)
             for y in range(0, cy, 8):
                 step(node, 0, y, False)
 
@@ -337,7 +340,11 @@
         copy.start()
         return copy
 
-    def send_y(stage):
+    def send_y(stage, sign):
+        for number, (sx, sy) in enumerate(CORNERS):
+            k = Y_GROUP[sy * sign].index(CORNER_POP[(sx * sign, sy * sign)])
+            row = pl.ds(cx - 1 if sx > 0 else 0, 1)
+            c_send[stage, number, :, :] = y_send[stage, 0 if sy > 0 else 1, k, row, :]
         copies = [
             send(stage, which, y_send.at[stage, which], y_recv.at[stage, which], 0, side)
             for which, side in enumerate((1, -1))
@@ -376,14 +383,13 @@
             buffer[POS[i], pl.ds(row, 1), :] = c_recv[stage, number]
 
     names[...] = jnp.zeros_like(names)
-    for load in loads[:5]:
+    for load in loads[:6]:
         load.wait()
+    y_edges(step_one, cx)
+    pl.semaphore_wait(barrier, n - 1)
+    copies = send_y(0, 1)
     x_faces(step_one)
-    pl.semaphore_wait(barrier, n - 1)
-    copies = send_x(0, ahead, 1)
-    loads[5].wait()
-    y_edges(step_one, cx)
-    copies += send_y(0)
+    copies += send_x(0, ahead, 1)
     inner(step_one, 1, cx - 1)
     for load in loads[6:]:
         load.wait()
@@ -393,7 +399,7 @@
     inner(step_two, 1, cx // 2)
     receive(0, copies, ahead, 1)
     y_edges(step_two, cx)
-    later = send_y(1)
+    later = send_y(1, -1)
     x_faces(step_two)
     later += send_x(1, behind, -1)
     inner(step_two, cx // 2, cx - 1)
@@ -423,16 +429,11 @@
     message[0] = note
     gathered[0] = note
 
-    def patch_copy(k):
-        return pltpu.make_async_remote_copy(
-            src_ref=message.at[0], dst_ref=gathered.at[k],
-            send_sem=patch_send, recv_sem=patch_recv,
-            device_id=place(k), device_id_type=MESH,
-        )
-
-    @pl.loop(1, n)
-    def _(k):
-        patch_copy(k).start()
+    for_others(lambda dx, dy: pltpu.make_async_remote_copy(
+        src_ref=message.at[0], dst_ref=gathered.at[dx * n_gy + dy],
+        send_sem=patch_send, recv_sem=patch_recv,
+        device_id=near(dx, dy), device_id_type=MESH,
+    ).start())
 
     y_edges(step_out, cx // 2)
     x_faces(step_out)
@@ -468,7 +469,8 @@
         names = jnp.where(low, one_turned, two) - base
         return total + jnp.where(names == patch, values, 0.0)
 
-    total = lax.fori_loop(0, n // 2, add, jnp.zeros((PATCH_DEV, nz), jnp.float32))
+    total = jnp.zeros((PATCH_DEV, nz), jnp.float32)
+    total = lax.fori_loop(0, n // 2, add, total, unroll=8)
     summed = lax.dot_general(
         jnp.ones((8, nz), jnp.float32), total, (((1,), (1,)), ((), ())),
         precision=lax.Precision.HIGHEST, preferred_element_type=jnp.float32,

time: 24.6 us -> 24.2 us (0.984)
  Pallas kernels: 23.8 us -> 23.4 us
    pallas_call x1, Pallas kernels: 2.37 us -> 1.48 us  [body(): pl.pallas_call(partial(finish, shape), out_shape=(whole, jax.ShapeDtypeSt...]
    pallas_call x1, Pallas kernels: 21.5 us -> 22 us  [body(): pl.pallas_call(partial(kernel, shape), out_shape=(whole, jax.ShapeDtypeSt...]
where the time goes in v3:
time: 24.2 us; the launch traced here: 24.1 us
  Pallas kernels  23.4 us (97%)
  between operations  0.64 us (3%)
    pallas_call x1, Pallas kernels, body(): pl.pallas_call(partial(kernel, shape), out_shape=(whole, jax.ShapeDtypeSt...  22 us
    pallas_call x1, Pallas kernels, body(): pl.pallas_call(partial(finish, shape), out_shape=(whole, jax.ShapeDtypeSt...  1.48 us

profile of v3, /device:TPU:0, one launch (start us, length us, event | category | flops | bytes accessed | tf_op | source)
XLA Modules:
  0.0 24.1 jit_solution(10198253293708271293)
XLA Ops:
  0.6 22.0 %shard_map.86 = (f32[19,256,128]{2,1,0:T(8,128)S(1)}, f32[32,1,128]{2,1,0:T(1,128)S(1)}) custom-call(f32[19,256,128]{2,1,0:T(8,128)} %bitcast.9, f32[256,128]{1,0:T(8,128)} %bitcast.11, f32[19,256,128]{2,1,0:T(8,128)} %bitcast.10, s32[256,128]{1,0:T(8,128)} %bitcast.12, s32[256,128]{1,0:T(8,128)} %bitcast.13, s32[1,64]{1,0:T(1,128)} %bitcast.14, ...), custom_call_target="tpu_custom_call" | custom-call | tf_op jit(solution)/shard_map/pallas_call | solution.py:500
  22.6 1.5 %shard_map.87 = (f32[19,256,128]{2,1,0:T(8,128)}, f32[1,256]{1,0:T(1,128)}) custom-call(f32[19,256,128]{2,1,0:T(8,128)S(1)} %get-tuple-element.6.result, f32[32,1,128]{2,1,0:T(1,128)S(1)} %get-tuple-element.7.gathered), custom_call_target="tpu_custom_call" | custom-call | tf_op jit(solution)/shard_map/pallas_call | solution.py:537

commit v4 on v3

--- a/solution.py
+++ b/solution.py
@@ -191,10 +191,7 @@
     stride = cy + 16
     gx, gy = lax.axis_index("gx"), lax.axis_index("gy")
 
-    faces = [pl.ds(0, cy), pl.ds((cx - 1) * cy, cy)]
-    middle = pl.ds(cy, (cx - 2) * cy)
-    pairs = [(porosity_hbm, porosity), (porous_hbm, porous), (walls_hbm, walls)]
-    pairs += [(pops_hbm.at[:, part, :], pops.at[:, part, :]) for part in faces + [middle]]
+    pairs = [(pops_hbm, pops), (porosity_hbm, porosity), (porous_hbm, porous), (walls_hbm, walls)]
     pairs += [(adj_hbm, adj), (owners_hbm, owners), (slots_hbm, slots)]
     loads = [
         pltpu.make_async_copy(src, dst, load_sem.at[k]) for k, (src, dst) in enumerate(pairs)
@@ -383,7 +380,7 @@
             buffer[POS[i], pl.ds(row, 1), :] = c_recv[stage, number]
 
     names[...] = jnp.zeros_like(names)
-    for load in loads[:6]:
+    for load in loads[:4]:
         load.wait()
     y_edges(step_one, cx)
     pl.semaphore_wait(barrier, n - 1)
@@ -391,7 +388,7 @@
     x_faces(step_one)
     copies += send_x(0, ahead, 1)
     inner(step_one, 1, cx - 1)
-    for load in loads[6:]:
+    for load in loads[4:]:
         load.wait()
     names[pl.ds(0, 1), pl.ds(0, owners.shape[1])] = (
         owners[...] * PATCH_DEV + slots[...]
@@ -419,13 +416,8 @@
         rows_of.append(part)
     blocks = (cx // 2) * (cy // 2)
     rows_of.append(jnp.zeros((nz - blocks, nz), jnp.float32))
-    contract = (((1,), (1,)), ((), ()))
-    ones = jnp.ones((8, nz), jnp.float32)
-    sums = lax.dot_general(
-        ones, jnp.concatenate(rows_of, axis=0), contract,
-        precision=lax.Precision.HIGHEST, preferred_element_type=jnp.float32,
-    )
-    note = sums[0:1, :] + pltpu.roll(names[...], nz // 2, 1)[0:1, :]
+    sums = jnp.sum(jnp.concatenate(rows_of, axis=0).T, axis=0, keepdims=True)
+    note = sums + pltpu.roll(names[...], nz // 2, 1)[0:1, :]
     message[0] = note
     gathered[0] = note
 
@@ -522,7 +514,7 @@
             pltpu.VMEM((2, 4, 1, nz), f32),
             pltpu.VMEM((1, 1, nz), f32),
             pltpu.VMEM((8, nz), f32),
-            pltpu.SemaphoreType.DMA((9,)),
+            pltpu.SemaphoreType.DMA((7,)),
             pltpu.SemaphoreType.DMA((2, 8)),
             pltpu.SemaphoreType.DMA((2, 8)),
             pltpu.SemaphoreType.DMA,

time: 24.2 us -> 23.9 us (0.988)
  Pallas kernels: 23.4 us -> 23.1 us
    pallas_call x1, Pallas kernels: 22 us -> 21.6 us  [body(): pl.pallas_call(partial(kernel, shape), out_shape=(whole, jax.ShapeDtypeSt...]
where the time goes in v4:
time: 23.9 us; the launch traced here: 23.7 us
  Pallas kernels  23.1 us (97%)
  between operations  0.64 us (3%)
    pallas_call x1, Pallas kernels, body(): pl.pallas_call(partial(kernel, shape), out_shape=(whole, jax.ShapeDtypeSt...  21.6 us
    pallas_call x1, Pallas kernels, body(): pl.pallas_call(partial(finish, shape), out_shape=(whole, jax.ShapeDtypeSt...  1.48 us

profile of v4, /device:TPU:0, one launch (start us, length us, event | category | flops | bytes accessed | tf_op | source)
XLA Modules:
  0.0 23.7 jit_solution(1749930464109211938)
XLA Ops:
  0.6 21.6 %shard_map.86 = (f32[19,256,128]{2,1,0:T(8,128)S(1)}, f32[32,1,128]{2,1,0:T(1,128)S(1)}) custom-call(f32[19,256,128]{2,1,0:T(8,128)} %bitcast.9, f32[256,128]{1,0:T(8,128)} %bitcast.11, f32[19,256,128]{2,1,0:T(8,128)} %bitcast.10, s32[256,128]{1,0:T(8,128)} %bitcast.12, s32[256,128]{1,0:T(8,128)} %bitcast.13, s32[1,64]{1,0:T(1,128)} %bitcast.14, ...), custom_call_target="tpu_custom_call" | custom-call | tf_op jit(solution)/shard_map/pallas_call | solution.py:492
  22.2 1.5 %shard_map.87 = (f32[19,256,128]{2,1,0:T(8,128)}, f32[1,256]{1,0:T(1,128)}) custom-call(f32[19,256,128]{2,1,0:T(8,128)S(1)} %get-tuple-element.6.result, f32[32,1,128]{2,1,0:T(1,128)S(1)} %get-tuple-element.7.gathered), custom_call_target="tpu_custom_call" | custom-call | tf_op jit(solution)/shard_map/pallas_call | solution.py:529
